TPU v7x, 256 devices: a whole 4x4x8 slice. The times are simulated.
256 devices in a mesh: dp: 64 (over z, x, core), group: 4 (over y).
Axes of the slice: x: 4, y: 4, z: 8, core: 2. Of those that a mesh axis runs over, the one named last changes fastest.
Arguments:
- frames: bfloat16 [64, 4, 384, 8192], P('dp', 'group'), may hold values from -6 to 6
- lengths: int32 [64, 4, 4], P('dp', 'group'), may hold values from 32 to 96, as said below
- probes: bfloat16 [8192, 256], P('dp'), may hold values from -0.0625 to 0.0625
Outputs:
- basis: float32 [8192, 256], P('dp')
- factor: float32 [256, 256], replicated
Inputs may be any that keep to these rules, and one draw needn't show every extreme that they name: `lengths`: each device's spans lie back to back from its first frame slot; the device at index 0 of both axes has all 4 spans of length 96.
All inputs are finite; a program needn't handle non-finite values.
Results may differ from a plain program's by a relative error of at most 0.0031.
Values may be sent and summed in bfloat16 or wider, within the bound.
A program may use at most 128 MiB of HBM per device.

v0:
```python
import math

import jax
import jax.numpy as jnp
from jax import lax
from jax.sharding import PartitionSpec as P


def pair_mask(lengths, count):
    ends = jnp.cumsum(lengths)
    starts = ends - lengths
    position = jnp.arange(count, dtype=jnp.int32)
    inside = (position[:, None] >= starts[None, :] + 1) & (position[:, None] <= ends[None, :] - 1)
    return jnp.any(inside, axis=1)


def shards(frames, lengths, probes):
    local = frames.reshape(frames.shape[2], frames.shape[3])
    sizes = lengths.reshape(lengths.shape[2])
    count = local.shape[0]
    width = local.shape[1]
    columns = probes.shape[1]
    devices = lax.axis_size("dp") * lax.axis_size("group")
    scale = 1.0 / math.sqrt(width * count * devices)
    cols = local
    projected = jnp.dot(
        cols, lax.all_gather(probes, "dp", axis=0, tiled=True), preferred_element_type=jnp.float32
    ).astype(jnp.bfloat16)
    shifted = jnp.concatenate([jnp.zeros((1, columns), jnp.bfloat16), projected[:-1]], axis=0)
    paired = jnp.where(pair_mask(sizes, count)[:, None], shifted, jnp.zeros_like(shifted))
    contract = (((0,), (0,)), ((), ()))
    cols = local
    owned = lax.psum_scatter(
        scale * lax.dot_general(cols, paired, contract, preferred_element_type=jnp.float32),
        "dp",
        scatter_dimension=0,
        tiled=True,
    )
    sketch = lax.psum(owned, "group")
    local_gram = jnp.dot(sketch.T, sketch, precision=lax.Precision.HIGHEST)
    gram = lax.psum(local_gram, "dp")
    lower = jnp.linalg.cholesky(gram)
    basis = jax.scipy.linalg.solve_triangular(lower, sketch.T, lower=True).T * math.sqrt(width)
    return (basis, lower.T)


def solution(mesh):
    placed = (P("dp", "group", None, None), P("dp", "group", None), P("dp", None))
    return jax.shard_map(
        shards, mesh=mesh, in_specs=placed, out_specs=(P("dp", None), P()), check_vma=False
    )
```

profile of v0, /device:TPU:1, one launch (start us, length us, event | category | flops | bytes accessed | tf_op | source)
XLA Modules:
  0.0 553.6 jit_solution(10978117318791723454)
XLA Ops:
  7.2 0.0 all-gather.2.cloned.1.call-start
  7.2 0.7 all-gather.2.cloned.1.call-update
  7.9 0.0 reduce-scatter.2.cloned.1.call-start
  7.9 0.8 reduce-window.7
  8.8 0.7 fusion.21
  9.4 0.1 fusion.20
  9.5 84.5 %all-gather.2.cloned.1.call-done = bf16[8192,256]{1,0:T(8,128)(2,1)} async-done(((bf16[128,256]{1,0:T(8,128)(2,1)}), bf16[8192,256]{1,0:T(8,128)(2,1)}) %all-gather.2.cloned.1.call-update) | async-done | bytes 4194320 | tf_op jit(solution)/shard_map/all_gather | solution.py:27
  94.0 0.0 copy-start
  94.0 5.9 %fusion.2 = bf16[384,256]{1,0:T(8,128)(2,1)S(1)} fusion(bf16[8192,256]{1,0:T(8,128)(2,1)} %all-gather.2.cloned.1.call-done, bf16[1,1,384,8192]{3,2,1,0:T(8,128)(2,1)} %param.3), kind=kOutput, calls=%fused_computation.5 | convolution fusion | flops 1610612736 | bytes 10682368 | tf_op jit(solution)/shard_map/dot_general | solution.py:26
  99.9 0.0 copy-done
  99.9 5.7 %fusion = f32[8192,256]{0,1:T(8,128)} fusion(bf16[1,1,384,8192]{3,2,1,0:T(8,128)(2,1)S(1)} %copy-done, bf16[383,256]{1,0:T(8,128)(2,1)S(1)} %bitcast.57, pred[384]{0:T(512)(128)(4,1)S(1)} %fusion.20), kind=kOutput, calls=%fused_computation.3 | convolution fusion | flops 1612808192 | bytes 14876544 | tf_op jit(solution)/shard_map/dot_general | solution.py:34
  105.6 0.0 reduce-scatter.2.cloned.1.call-update
  105.6 0.0 all-reduce.5.cloned.1.call-start
  105.7 143.7 %reduce-scatter.2.cloned.1.call-done = f32[128,256]{0,1:T(8,128)} async-done(((f32[8192,256]{0,1:T(8,128)}), f32[128,256]{0,1:T(8,128)}) %reduce-scatter.2.cloned.1.call-update) | async-done | bytes 131088 | tf_op jit(solution)/shard_map/reduce_scatter | solution.py:33
  249.4 0.0 all-reduce.5.cloned.1.call-update
  249.4 0.2 all-reduce.7.cloned.1.call-start
  249.6 49.4 %all-reduce.5.cloned.1.call-done = f32[128,256]{0,1:T(8,128)} async-done(((f32[128,256]{0,1:T(8,128)}), f32[128,256]{0,1:T(8,128)}) %all-reduce.5.cloned.1.call-update) | async-done | bytes 131088 | tf_op jit(solution)/shard_map/psum | solution.py:39
  299.0 2.1 fusion.24
  301.1 0.0 all-reduce.7.cloned.1.call-update
  301.2 179.8 %all-reduce.7.cloned.1.call-done = f32[256,256]{0,1:T(8,128)} async-done(((f32[256,256]{0,1:T(8,128)}), f32[256,256]{0,1:T(8,128)}) %all-reduce.7.cloned.1.call-update) | async-done | bytes 262160 | tf_op jit(solution)/shard_map/psum | solution.py:41
  480.9 1.1 copy.10
  482.0 1.0 fusion.4
  483.0 11.7 %cholesky.50 = f32[128,128]{1,0:T(8,128)S(1)} custom-call(f32[128,128]{1,0:T(8,128)S(1)} %cholesky.118), custom_call_target="Cholesky" | custom-call | tf_op jit(solution)/shard_map/jit(cholesky)/cholesky | solution.py:42
  494.8 9.8 %custom-call.15 = f32[1,128,128]{1,2,0:T(8,128)S(1)} custom-call(f32[1,128,128]{2,1,0:T(8,128)S(1)} %get-tuple-element.29), custom_call_target="InvertDiagBlocksLowerTriangular" | custom-call | tf_op jit(solution)/shard_map/jit(cholesky)/cholesky | solution.py:42
  504.6 0.2 constant_dynamic-update-slice_fusion.1
  504.8 0.3 convolution_subtract_fusion.1
  505.1 11.7 %cholesky.105 = f32[128,128]{1,0:T(8,128)S(1)} custom-call(f32[128,128]{1,0:T(8,128)S(1)} %convolution_subtract_fusion.1), custom_call_target="Cholesky" | custom-call | tf_op jit(solution)/shard_map/jit(cholesky)/cholesky | solution.py:42
  516.9 0.7 compare_reduce_fusion
  519.0 0.1 triangular_solve.57
  519.0 4.3 while.1
  519.2 0.6 fusion.33
  519.8 1.4 bitcast_dynamic-update-slice_fusion.2
  521.3 0.6 fusion.33
  521.9 1.4 bitcast_dynamic-update-slice_fusion.2
  523.3 19.7 %custom-call.16 = f32[2,128,128]{1,2,0:T(8,128)S(1)} custom-call(f32[2,128,128]{2,1,0:T(8,128)S(1)} %get-tuple-element.9), custom_call_target="InvertDiagBlocksLowerTriangular" | custom-call | tf_op jit(solution)/shard_map/jit(_solve_triangular)/triangular_solve | solution.py:43
  543.0 1.1 fusion.14
  544.1 1.0 convolution_subtract_fusion
  545.2 0.3 fusion.13
  545.5 0.8 copy.11
  546.3 0.8 copy.12
  (10 shorter events, 0.2 us)
Async XLA Ops:
  7.2 86.8 %all-gather.2.cloned.1.call-start = ((), (), s32[]{:S(2)}) async-start(), calls=%async_computation.1 | async-start | bytes 4259840 | tf_op jit(solution)/shard_map/all_gather | solution.py:27
  7.9 241.5 %reduce-scatter.2.cloned.1.call-start = ((), (), s32[]{:S(2)}) async-start(), calls=%async_computation.2 | async-start | bytes 8519680 | tf_op jit(solution)/shard_map/reduce_scatter | solution.py:33
  94.0 5.9 %copy-start = (bf16[1,1,384,8192]{3,2,1,0:T(8,128)(2,1)S(1)}, bf16[1,1,384,8192]{3,2,1,0:T(8,128)(2,1)}, u32[]{:S(2)}) copy-start(bf16[1,1,384,8192]{3,2,1,0:T(8,128)(2,1)} %param.3) | copy-start | bytes 18874372
  105.6 193.4 %all-reduce.5.cloned.1.call-start = ((), (), s32[]{:S(2)}) async-start(), calls=%async_computation.3 | async-start | bytes 262144 | tf_op jit(solution)/shard_map/psum | solution.py:39
  249.4 231.5 %all-reduce.7.cloned.1.call-start = ((), (), s32[]{:S(2)}) async-start(), calls=%async_computation.4 | async-start | bytes 524288 | tf_op jit(solution)/shard_map/psum | solution.py:41
Sparse Core Ops, SparseCore 0:
  10.8 83.1 all-gather.1
  105.8 143.5 reduce-scatter.1
  251.8 47.1 all-reduce.4
  302.9 177.9 all-reduce.6
where the time goes:
time: 554 us
  waiting for transfers between devices  458 us (83%)
  other arithmetic  56.3 us (10%)
  matrix products  16.6 us (3%)
  between operations  15.2 us (3%)
  local copies, waits for them, and re-layouts  6.83 us (1%)
    psum x1, waiting for transfers between devices, shards(): gram = lax.psum(local_gram, 'dp')  180 us
    reduce_scatter x1, waiting for transfers between devices, shards(): lax.psum_scatter(scale * lax.dot_general(cols, paired, contract, preferre...  144 us
    all_gather x1, waiting for transfers between devices, shards(): lax.all_gather(probes, 'dp', axis=0, tiled=True)  84.5 us
    psum x1, waiting for transfers between devices, shards(): sketch = lax.psum(owned, 'group')  49.4 us
    another operation x6, other arithmetic, shards(): lower = jnp.linalg.cholesky(gram)  34 us
    another operation x2, other arithmetic, shards(): jax.scipy.linalg.solve_triangular(lower, sketch.T, lower=True)  19.7 us
  transfers between devices with their start and end apart: 4, of which 4 were waited for; matrix products, arithmetic and copies ran while one was open for 0% of the time, Pallas kernels for 0%

commit v1 on v0

v1 whole, which is shorter than its diff:
```python
import functools
import math

import jax
import jax.numpy as jnp
from jax import lax
from jax.experimental import pallas as pl
from jax.experimental.pallas import tpu as pltpu
from jax.sharding import PartitionSpec as P

MESH = pl.DeviceIdType.MESH
NZ, NX, NY, NC = 8, 4, 4, 2
NXY = NX * NY
NXYC = NXY * NC
BLOCK = 128
PIECE = BLOCK // NY


def device(z, x, c, y):
    return ((z * NX + x) * NC + c, y)


def remote(src, dst, send, recv, where):
    return pltpu.make_async_remote_copy(
        src_ref=src,
        dst_ref=dst,
        send_sem=send,
        recv_sem=recv,
        device_id=where,
        device_id_type=MESH,
    )


def kernel(
    scale,
    lens,
    frames,
    probes,
    sketch_ref,
    gram_ref,
    w,
    wt,
    pb,
    masks,
    part,
    other,
    paired,
    tsend,
    trecv,
    rows,
    zrecv,
    local_sem,
    probe_sem,
    frame_sems,
    mask_sems,
    part_sems,
    az_s,
    az_r,
    ap_s,
    ap_r,
    rs_s,
    rs_r,
    rz_s,
    rz_r,
    y_s,
    y_r,
    gsend,
    grecv,
    gz,
    g_s,
    g_r,
    gz_s,
    gz_r,
    ga_s,
    ga_r,
):
    dp = lax.axis_index("dp")
    y = lax.axis_index("group")
    c = dp % NC
    x = (dp // NC) % NX
    z = dp // (NC * NX)
    count = frames.shape[0]

    def at_z(k):
        return device((z + k) % NZ, x, c, y)

    def at_xy(k):
        return (x + k // NY) % NX, (y + k % NY) % NY

    def dev_xy(k):
        px, py = at_xy(k)
        return device(z, px, c, py)

    def at_xyc(k):
        return (x + k // (NY * NC)) % NX, (y + (k // NC) % NY) % NY, (c + k % NC) % NC

    def dev_xyc(k):
        px, py, pc = at_xyc(k)
        return device(z, px, pc, py)

    partner = device(z, x, 1 - c, y)

    def own(i, _):
        col = ((i % NZ) * NX + i // NZ) * NC + c
        pltpu.make_async_copy(
            frames.at[:, pl.ds(pl.multiple_of(col * BLOCK, BLOCK), BLOCK)],
            w.at[pl.ds(pl.multiple_of(c * count, 128), count), pl.ds(pl.multiple_of(i * BLOCK, BLOCK), BLOCK)],
            local_sem,
        ).start()
        return 0

    mine = pltpu.make_async_copy(
        probes.at[pl.ds(pl.multiple_of(y * PIECE, PIECE), PIECE)], pb.at[x, z, y], probe_sem
    )
    mine.start()
    lax.fori_loop(0, NZ * NX, own, 0)

    barrier = pltpu.get_barrier_semaphore()

    def greet_z(k, _):
        pl.semaphore_signal(barrier, inc=1, device_id=at_z(k), device_id_type=MESH)
        return 0

    def greet_xyc(k, _):
        pl.semaphore_signal(barrier, inc=1, device_id=dev_xyc(k), device_id_type=MESH)
        return 0

    lax.fori_loop(1, NZ, greet_z, 0)
    lax.fori_loop(1, NXYC, greet_xyc, 0)

    position = lax.broadcasted_iota(jnp.int32, (count, BLOCK), 0)
    inside = jnp.zeros((count, BLOCK), jnp.float32)
    start = jnp.int32(0)
    for span in range(4):
        end = start + lens[0, 0, span]
        inside = inside + jnp.where(
            jnp.logical_and(position >= start + 1, position <= end - 1), 1.0, 0.0
        )
        start = end
    masks[c] = inside

    pl.semaphore_wait(barrier, NZ - 1 + NXYC - 1)

    mine.wait()

    def gather_z(k):
        return remote(pb.at[x, z, y], pb.at[x, z, y], az_s.at[k], az_r.at[k], at_z(k))

    def start_gather_z(k, _):
        gather_z(k).start()
        return 0

    lax.fori_loop(1, NZ, start_gather_z, 0)

    def give(i, _):
        col = ((i % NZ) * NX + i // NZ) * NC + (1 - c)
        remote(
            frames.at[:, pl.ds(pl.multiple_of(col * BLOCK, BLOCK), BLOCK)],
            w.at[pl.ds(pl.multiple_of(c * count, 128), count), pl.ds(pl.multiple_of(i * BLOCK, BLOCK), BLOCK)],
            frame_sems.at[0],
            frame_sems.at[1],
            partner,
        ).start()
        return 0

    lax.fori_loop(0, NZ * NX, give, 0)
    mask_copy = remote(masks.at[c], masks.at[c], mask_sems.at[0], mask_sems.at[1], partner)
    mask_copy.start()

    def wait_gather_z(k, _):
        gather_z(k).wait()
        return 0

    lax.fori_loop(1, NZ, wait_gather_z, 0)

    def gather_xy(k):
        return remote(pb.at[x, :, y], pb.at[x, :, y], ap_s.at[k], ap_r.at[k], dev_xy(k))

    def start_gather_xy(k, _):
        gather_xy(k).start()
        return 0

    lax.fori_loop(1, NXY, start_gather_xy, 0)

    mine_rows = w.at[pl.ds(pl.multiple_of(c * count, 128), count)]
    pltpu.make_async_copy(mine_rows, mine_rows, local_sem).wait()
    frames_copy = remote(mine_rows, mine_rows, frame_sems.at[0], frame_sems.at[1], partner)
    frames_copy.wait()
    mask_copy.wait()

    def turn(i, _):
        block = w[:, pl.ds(pl.multiple_of(i * BLOCK, BLOCK), BLOCK)]
        wt[i // NZ, i % NZ] = block.T.reshape(NY, PIECE, 2 * count)
        return 0

    lax.fori_loop(0, NZ * NX, turn, 0)

    def project(dx, _):
        def arrived(dy, _):
            gather_xy(dx * NY + dy).wait_recv()
            return 0

        lax.fori_loop(jnp.where(dx == 0, 1, 0), NY, arrived, 0)
        px = (x - dx + NX) % NX
        depth = NZ * BLOCK
        block = pb[px].reshape(depth, pb.shape[-1])
        product = jnp.dot(
            w[:, pl.ds(pl.multiple_of(px * depth, depth), depth)],
            block,
            preferred_element_type=jnp.float32,
        )

        @pl.when(dx == 0)
        def _():
            part[...] = product

        @pl.when(dx > 0)
        def _():
            part[...] += product

        return 0

    lax.fori_loop(0, NX, project, 0)

    swap = remote(part, other, part_sems.at[0], part_sems.at[1], partner)
    swap.start()
    swap.wait()
    shifted = pltpu.roll(part[...] + other[...], 1, 0)
    mask = masks[...].reshape(2 * count, BLOCK)
    mask = jnp.concatenate([mask, mask], axis=1)
    paired[...] = jnp.where(mask > 0.5, shifted, 0.0).astype(jnp.bfloat16)

    def term(px, py):
        lhs = wt[px, :, py].reshape(NZ * PIECE, 2 * count)
        return jnp.dot(lhs, paired[...], preferred_element_type=jnp.float32)

    def scatter_xy(k):
        return remote(tsend.at[k], trecv.at[k], rs_s.at[k], rs_r.at[k], dev_xy(k))

    def start_scatter_xy(k, _):
        px, py = at_xy(k)
        tsend[k] = term(px, py).astype(jnp.bfloat16)
        scatter_xy(k).start()
        return 0

    lax.fori_loop(1, NXY, start_scatter_xy, 0)
    rows[...] = term(x, y)

    def sum_xy(k, _):
        scatter_xy(k).wait_recv()
        rows[...] += trecv[k].astype(jnp.float32)
        return 0

    lax.fori_loop(1, NXY, sum_xy, 0)

    def scatter_z(k):
        there = (z + k) % NZ
        return remote(
            rows.at[pl.ds(pl.multiple_of(there * PIECE, PIECE), PIECE)],
            zrecv.at[k],
            rz_s.at[k],
            rz_r.at[k],
            at_z(k),
        )

    def start_scatter_z(k, _):
        scatter_z(k).start()
        return 0

    lax.fori_loop(1, NZ, start_scatter_z, 0)
    total = rows[pl.ds(pl.multiple_of(z * PIECE, PIECE), PIECE)]

    def sum_z(k, total):
        scatter_z(k).wait_recv()
        return total + zrecv[k]

    total = lax.fori_loop(1, NZ, sum_z, total) * scale
    here = pl.ds(pl.multiple_of(y * PIECE, PIECE), PIECE)
    sketch_ref[here] = total

    def gather_y(k):
        return remote(
            sketch_ref.at[here],
            sketch_ref.at[here],
            y_s.at[k],
            y_r.at[k],
            device(z, x, c, (y + k) % NY),
        )

    gsend[...] = jnp.dot(
        total.T, total, preferred_element_type=jnp.float32, precision=lax.Precision.HIGHEST
    ).reshape(gsend.shape)

    def scatter_g(k):
        px, py, pc = at_xyc(k)
        return remote(
            gsend.at[(px * NY + py) * NC + pc], grecv.at[k], g_s.at[k], g_r.at[k], dev_xyc(k)
        )

    def start_scatter_g(k, _):
        scatter_g(k).start()
        return 0

    lax.fori_loop(1, NXYC, start_scatter_g, 0)

    def start_gather_y(k, _):
        gather_y(k).start()
        return 0

    lax.fori_loop(1, NY, start_gather_y, 0)
    me = (x * NY + y) * NC + c

    def sum_g(k, acc):
        scatter_g(k).wait_recv()
        return acc + grecv[k]

    gz[z] = lax.fori_loop(1, NXYC, sum_g, gsend[me])

    def spread_z(k):
        return remote(gz.at[z], gz.at[z], gz_s.at[k], gz_r.at[k], at_z(k))

    def start_spread_z(k, _):
        spread_z(k).start()
        return 0

    def wait_spread_z(k, _):
        spread_z(k).wait()
        return 0

    lax.fori_loop(1, NZ, start_spread_z, 0)
    lax.fori_loop(1, NZ, wait_spread_z, 0)
    acc = gz[0]
    for k in range(1, NZ):
        acc = acc + gz[k]
    gram_ref[me] = acc

    def gather_g(k):
        return remote(gram_ref.at[me], gram_ref.at[me], ga_s.at[k], ga_r.at[k], dev_xyc(k))

    def start_gather_g(k, _):
        gather_g(k).start()
        return 0

    def wait_gather_g(k, _):
        gather_g(k).wait()
        return 0

    lax.fori_loop(1, NXYC, start_gather_g, 0)

    def end_xy(k, _):
        gather_xy(k).wait_send()
        scatter_xy(k).wait_send()
        return 0

    def end_z(k, _):
        scatter_z(k).wait_send()
        return 0

    def end_g(k, _):
        scatter_g(k).wait_send()
        return 0

    def end_y(k, _):
        gather_y(k).wait()
        return 0

    lax.fori_loop(1, NXY, end_xy, 0)
    lax.fori_loop(1, NZ, end_z, 0)
    lax.fori_loop(1, NXYC, end_g, 0)
    lax.fori_loop(1, NY, end_y, 0)
    lax.fori_loop(1, NXYC, wait_gather_g, 0)


def sketch_and_gram(frames, lengths, probes, devices):
    count, width = frames.shape
    columns = probes.shape[1]
    scale = 1.0 / math.sqrt(width * count * devices)
    half = width // NC
    dma = pltpu.SemaphoreType.DMA
    f32, bf16 = jnp.float32, jnp.bfloat16
    return pl.pallas_call(
        functools.partial(kernel, scale),
        out_shape=(
            jax.ShapeDtypeStruct((BLOCK, columns), f32),
            jax.ShapeDtypeStruct((NXYC, columns // NXYC, columns), f32),
        ),
        in_specs=[
            pl.BlockSpec(memory_space=pltpu.SMEM),
            pl.BlockSpec(memory_space=pl.ANY),
            pl.BlockSpec(memory_space=pl.ANY),
        ],
        out_specs=(pl.BlockSpec(memory_space=pltpu.VMEM), pl.BlockSpec(memory_space=pltpu.VMEM)),
        scratch_shapes=[
            pltpu.VMEM((NC * count, half), bf16),
            pltpu.VMEM((NX, NZ, NY, PIECE, NC * count), bf16),
            pltpu.VMEM((NX, NZ, NY, PIECE, columns), bf16),
            pltpu.VMEM((NC, count, BLOCK), f32),
            pltpu.VMEM((NC * count, columns), f32),
            pltpu.VMEM((NC * count, columns), f32),
            pltpu.VMEM((NC * count, columns), bf16),
            pltpu.VMEM((NXY, NZ * PIECE, columns), bf16),
            pltpu.VMEM((NXY, NZ * PIECE, columns), bf16),
            pltpu.VMEM((NZ * PIECE, columns), f32),
            pltpu.VMEM((NZ, PIECE, columns), f32),
            dma,
            dma,
            dma((2,)),
            dma((2,)),
            dma((2,)),
            dma((NZ,)),
            dma((NZ,)),
            dma((NXY,)),
            dma((NXY,)),
            dma((NXY,)),
            dma((NXY,)),
            dma((NZ,)),
            dma((NZ,)),
            dma((NY,)),
            dma((NY,)),
            pltpu.VMEM((NXYC, columns // NXYC, columns), f32),
            pltpu.VMEM((NXYC, columns // NXYC, columns), f32),
            pltpu.VMEM((NZ, columns // NXYC, columns), f32),
            dma((NXYC,)),
            dma((NXYC,)),
            dma((NZ,)),
            dma((NZ,)),
            dma((NXYC,)),
            dma((NXYC,)),
        ],
        compiler_params=pltpu.CompilerParams(
            collective_id=0, has_side_effects=True, vmem_limit_bytes=48 << 20
        ),
    )(lengths, frames, probes)


def shards(frames, lengths, probes):
    local = frames.reshape(frames.shape[2], frames.shape[3])
    width = local.shape[1]
    columns = probes.shape[1]
    devices = lax.axis_size("dp") * lax.axis_size("group")
    sketch, gram = sketch_and_gram(local, lengths, probes, devices)
    gram = gram.reshape(columns, columns)
    lower = jnp.linalg.cholesky(gram)
    basis = jax.scipy.linalg.solve_triangular(lower, sketch.T, lower=True).T * math.sqrt(width)
    return (basis, lower.T)


def solution(mesh):
    placed = (P("dp", "group", None, None), P("dp", "group", None), P("dp", None))
    return jax.shard_map(
        shards, mesh=mesh, in_specs=placed, out_specs=(P("dp", None), P()), check_vma=False
    )
```

time: 554 us -> 178 us (0.32)
  waiting for transfers between devices: 458 us -> 0 us
  Pallas kernels: 0 us -> 113 us
  matrix products: 16.6 us -> 1.33 us
  between operations: 15.2 us -> 2.07 us
    psum x2 -> x0, waiting for transfers between devices: 229 us -> none  [the longest x1 180 us: shards(): gram = lax.psum(local_gram, 'dp')]
    reduce_scatter x1 -> x0, waiting for transfers between devices: 144 us -> none  [shards(): lax.psum_scatter(scale * lax.dot_general(cols, paired, contract, preferre...]
    pallas_call x0 -> x1, Pallas kernels: none -> 113 us  [sketch_and_gram(): pl.pallas_call(functools.partial(kernel, scale), out_shape=(jax.ShapeDtyp...]
    all_gather x1 -> x0, waiting for transfers between devices: 84.5 us -> none  [shards(): lax.all_gather(probes, 'dp', axis=0, tiled=True)]
    dot_general x3 -> x0, matrix products: 13.7 us -> none  [the longest x1 5.94 us: shards(): jnp.dot(cols, lax.all_gather(probes, 'dp', axis=0, tiled=True), preferred...]
  transfers between devices with their start and end apart: 4 -> 0, of which waited for: 4 -> 0; matrix products, arithmetic and copies ran while one was open for 0% -> 0% of each run, Pallas kernels for 0% -> 0%
where the time goes in v1:
time: 178 us; the launch traced here: 177 us
  Pallas kernels  113 us (63%)
  other arithmetic  53.9 us (30%)
  local copies, waits for them, and re-layouts  7.36 us (4%)
  between operations  2.07 us (1%)
    pallas_call x1, Pallas kernels, sketch_and_gram(): pl.pallas_call(functools.partial(kernel, scale), out_shape=(jax.ShapeDtyp...  113 us
    another operation x6, other arithmetic, shards(): lower = jnp.linalg.cholesky(gram)  34 us
    another operation x2, other arithmetic, shards(): jax.scipy.linalg.solve_triangular(lower, sketch.T, lower=True)  19.9 us
    another operation x6, local copies, waits for them, and re-layouts  4.06 us

profile of v1, /device:TPU:1, one launch (start us, length us, event | category | flops | bytes accessed | tf_op | source)
XLA Modules:
  0.0 177.4 jit_solution(8817309816963092434)
XLA Ops:
  0.6 0.0 copy-start
  0.6 0.8 copy-done
  1.5 0.0 copy-start.1
  1.5 0.7 copy-done.1
  2.1 112.7 %shard_map.50 = (f32[128,256]{1,0:T(8,128)S(1)}, f32[32,8,256]{2,1,0:T(8,128)S(1)}) custom-call(s32[1,1,4]{2,1,0:T(1,128)S(1)} %copy-done.1, bf16[384,8192]{1,0:T(8,128)(2,1)} %bitcast.42, bf16[128,256]{1,0:T(8,128)(2,1)S(1)} %copy-done), custom_call_target="tpu_custom_call" | custom-call | tf_op jit(solution)/shard_map/pallas_call | solution.py:381
  114.9 0.1 copy.9
  115.1 11.7 %cholesky.50 = f32[128,128]{1,0:T(8,128)S(1)} custom-call(f32[128,128]{1,0:T(8,128)S(1)} %cholesky.118), custom_call_target="Cholesky" | custom-call | tf_op jit(solution)/shard_map/jit(cholesky)/cholesky | solution.py:443
  126.8 9.8 %custom-call.15 = f32[1,128,128]{1,2,0:T(8,128)S(1)} custom-call(f32[1,128,128]{2,1,0:T(8,128)S(1)} %get-tuple-element.33), custom_call_target="InvertDiagBlocksLowerTriangular" | custom-call | tf_op jit(solution)/shard_map/jit(cholesky)/cholesky | solution.py:443
  136.7 0.2 constant_dynamic-update-slice_fusion.1
  136.9 0.3 convolution_subtract_fusion.1
  137.1 11.7 %cholesky.105 = f32[128,128]{1,0:T(8,128)S(1)} custom-call(f32[128,128]{1,0:T(8,128)S(1)} %convolution_subtract_fusion.1), custom_call_target="Cholesky" | custom-call | tf_op jit(solution)/shard_map/jit(cholesky)/cholesky | solution.py:443
  148.9 0.6 compare_reduce_fusion
  150.9 0.1 triangular_solve.57
  151.0 4.1 %while.1 = (s32[]{:T(128)}, f32[256,256]{1,0:T(8,128)S(1)}, s32[2,2]{1,0:T(2,128)S(1)}, f32[2,128,128]{2,1,0:T(8,128)S(1)}, s32[]{:T(128)}) while((s32[]{:T(128)}, f32[256,256]{1,0:T(8,128)S(1)}, s32[2,2]{1,0:T(2,128)S(1)}, f32[2,128,128]{2,1,0:T(8,128)S(1)}, s32[]{:T(128)}) %tuple.30), condition=%wide.while_cond, body=%wide.while_body.sunk | while | flops 2 | bytes 131181 | solution.py:444
  151.0 0.6 fusion.17
  151.6 1.4 bitcast_dynamic-update-slice_fusion.2
  153.0 0.6 fusion.17
  153.6 1.4 bitcast_dynamic-update-slice_fusion.2
  155.1 19.9 %custom-call.16 = f32[2,128,128]{1,2,0:T(8,128)S(1)} custom-call(f32[2,128,128]{2,1,0:T(8,128)S(1)} %get-tuple-element.13), custom_call_target="InvertDiagBlocksLowerTriangular" | custom-call | tf_op jit(solution)/shard_map/jit(_solve_triangular)/triangular_solve | solution.py:444
  174.9 0.3 fusion.6
  175.2 0.3 convolution_subtract_fusion
  175.5 0.3 fusion.5
  175.8 0.8 copy.10
  176.6 0.8 copy.11
  (11 shorter events, 0.2 us)
Async XLA Ops:
  0.6 0.8 copy-start
  1.5 0.7 copy-start.1

commit v2 on v1

--- a/solution.py
+++ b/solution.py
@@ -433,6 +433,114 @@
     )(lengths, frames, probes)
 
 
+LANES = 128
+PANEL = 8
+
+
+def splat(v):
+    return lax.broadcast_in_dim(v, (PANEL, LANES), (0, 1))
+
+
+def less(x, y, z):
+    return lax.sub(x, lax.mul(y, z))
+
+
+def finish_kernel(scale, sketch, gram, basis, factor, a, b, inverse):
+    n = gram.shape[0]
+    panels = n // PANEL
+    lane_tiles = n // LANES
+    a[...] = gram[...]
+    b[...] = jnp.where(
+        lax.broadcasted_iota(jnp.int32, (n, n), 0) == lax.broadcasted_iota(jnp.int32, (n, n), 1),
+        1.0,
+        0.0,
+    )
+
+    def tile(ref, top, rows, t):
+        return ref.at[top : top + rows, t * LANES : (t + 1) * LANES]
+
+    one = jnp.ones((PANEL, LANES), jnp.float32)
+    for p in range(panels):
+        top = p * PANEL
+        first = top // LANES
+        tiles = [(a, t) for t in range(first, lane_tiles)] + [(b, t) for t in range(first + 1)]
+        many = range(len(tiles))
+        columns = [
+            splat(a[top : top + PANEL, top + j : top + j + 1])
+            for j in range(PANEL)
+        ]
+        d = [[splat(lax.slice(columns[j], (i, 0), (i + 1, LANES))) for j in range(i + 1)] for i in range(PANEL)]
+        rows = [[splat(tile(ref, top + i, 1, t)[...]) for ref, t in tiles] for i in range(PANEL)]
+        m = [[None] * PANEL for _ in range(PANEL)]
+        inv = [None] * PANEL
+        for j in range(PANEL):
+            inv[j] = lax.div(one, d[j][j])
+            for i in range(j + 1, PANEL):
+                m[i][j] = lax.mul(d[i][j], inv[j])
+            for i in range(j + 1, PANEL):
+                for k in range(j + 1, i + 1):
+                    d[i][k] = less(d[i][k], m[i][j], d[k][j])
+                for k in many:
+                    rows[i][k] = less(rows[i][k], m[i][j], rows[j][k])
+        w = [None] * PANEL
+        for i in reversed(range(PANEL)):
+            w[i] = []
+            for k in many:
+                acc = lax.mul(inv[i], rows[i][k])
+                for q in reversed(range(i + 1, PANEL)):
+                    acc = less(acc, m[q][i], w[q][k])
+                w[i].append(acc)
+
+        def update(below, _):
+            here = pl.ds(pl.multiple_of(below * PANEL, PANEL), PANEL)
+            v = [splat(a[here, top + j : top + j + 1]) for j in range(PANEL)]
+            for k, (ref, t) in enumerate(tiles):
+                block = ref.at[here, t * LANES : (t + 1) * LANES]
+                value = block[...]
+                for j in range(PANEL):
+                    value = less(value, v[j], w[j][k])
+                block[...] = value
+            return 0
+
+        if p + 1 < panels:
+            lax.fori_loop(p + 1, panels, update, 0, unroll=True)
+        for i in range(PANEL):
+            root = lax.rsqrt(d[i][i])
+            for t in range(lane_tiles):
+                upper = jnp.zeros((1, LANES), jnp.float32)
+                lower = upper
+                if t >= first:
+                    upper = (rows[i][t - first] * root)[0:1]
+                if t == first:
+                    lane = lax.broadcasted_iota(jnp.int32, (1, LANES), 1) + t * LANES
+                    upper = jnp.where(lane >= top + i, upper, 0.0)
+                if t <= first:
+                    lower = (rows[i][lane_tiles - first + t] * root)[0:1]
+                tile(factor, top + i, 1, t)[...] = upper
+                tile(inverse, top + i, 1, t)[...] = lower
+    basis[...] = scale * lax.dot_general(
+        sketch[...],
+        inverse[...],
+        (((1,), (1,)), ((), ())),
+        precision=lax.Precision.HIGHEST,
+        preferred_element_type=jnp.float32,
+    )
+
+
+def finish(sketch, gram, scale):
+    return pl.pallas_call(
+        functools.partial(finish_kernel, scale),
+        out_shape=(
+            jax.ShapeDtypeStruct(sketch.shape, jnp.float32),
+            jax.ShapeDtypeStruct(gram.shape, jnp.float32),
+        ),
+        in_specs=[pl.BlockSpec(memory_space=pltpu.VMEM)] * 2,
+        out_specs=(pl.BlockSpec(memory_space=pltpu.VMEM),) * 2,
+        scratch_shapes=[pltpu.VMEM(gram.shape, jnp.float32)] * 3,
+        compiler_params=pltpu.CompilerParams(vmem_limit_bytes=32 << 20),
+    )(sketch, gram)
+
+
 def shards(frames, lengths, probes):
     local = frames.reshape(frames.shape[2], frames.shape[3])
     width = local.shape[1]
@@ -440,9 +548,7 @@
     devices = lax.axis_size("dp") * lax.axis_size("group")
     sketch, gram = sketch_and_gram(local, lengths, probes, devices)
     gram = gram.reshape(columns, columns)
-    lower = jnp.linalg.cholesky(gram)
-    basis = jax.scipy.linalg.solve_triangular(lower, sketch.T, lower=True).T * math.sqrt(width)
-    return (basis, lower.T)
+    return finish(sketch, gram, math.sqrt(width))
 
 
 def solution(mesh):

time: 178 us -> 127 us (0.71)
  other arithmetic: 53.9 us -> 0 us
  Pallas kernels: 113 us -> 125 us
  local copies, waits for them, and re-layouts: 7.36 us -> 1.49 us
    another operation x8 -> x0, other arithmetic: 53.8 us -> none  [the longest x6 34 us: shards(): lower = jnp.linalg.cholesky(gram)]
    pallas_call x0 -> x1, Pallas kernels: none -> 12.1 us  [finish(): pl.pallas_call(functools.partial(finish_kernel, scale), out_shape=(jax.Sh...]
    another operation x9 -> x0, local copies, waits for them, and re-layouts: 4.16 us -> none
where the time goes in v2:
time: 127 us
  Pallas kernels  125 us (98%)
  local copies, waits for them, and re-layouts  1.49 us (1%)
    pallas_call x1, Pallas kernels, sketch_and_gram(): pl.pallas_call(functools.partial(kernel, scale), out_shape=(jax.ShapeDtyp...  113 us
    pallas_call x1, Pallas kernels, finish(): pl.pallas_call(functools.partial(finish_kernel, scale), out_shape=(jax.Sh...  12.1 us

profile of v2, /device:TPU:1, one launch (start us, length us, event | category | flops | bytes accessed | tf_op | source)
XLA Modules:
  0.0 126.9 jit_solution(11147324135431234583)
XLA Ops:
  0.6 0.0 copy-start
  0.6 0.8 copy-done
  1.5 0.0 copy-start.1
  1.5 0.7 copy-done.1
  2.1 112.7 %shard_map.50 = (f32[128,256]{1,0:T(8,128)S(1)}, f32[32,8,256]{2,1,0:T(8,128)S(1)}) custom-call(s32[1,1,4]{2,1,0:T(1,128)S(1)} %copy-done.1, bf16[384,8192]{1,0:T(8,128)(2,1)} %bitcast.3, bf16[128,256]{1,0:T(8,128)(2,1)S(1)} %copy-done), custom_call_target="tpu_custom_call" | custom-call | tf_op jit(solution)/shard_map/pallas_call | solution.py:381
  114.8 12.1 %shard_map.51 = (f32[128,256]{1,0:T(8,128)}, f32[256,256]{1,0:T(8,128)}) custom-call(f32[128,256]{1,0:T(8,128)S(1)} %get-tuple-element.4.sketch, f32[256,256]{1,0:T(8,128)S(1)} %bitcast.2), custom_call_target="tpu_custom_call" | custom-call | tf_op jit(solution)/shard_map/pallas_call | solution.py:531
Async XLA Ops:
  0.6 0.8 copy-start
  1.5 0.7 copy-start.1

commit v3 on v2

--- a/solution.py
+++ b/solution.py
@@ -14,6 +14,8 @@
 NXYC = NXY * NC
 BLOCK = 128
 PIECE = BLOCK // NY
+HALF = NZ // 2
+ORDER = (1, 3, 2)
 
 
 def device(z, x, c, y):
@@ -33,11 +35,12 @@
 
 def kernel(
     scale,
-    lens,
+    lengths,
     frames,
     probes,
     sketch_ref,
     gram_ref,
+    lens,
     w,
     wt,
     pb,
@@ -47,10 +50,14 @@
     paired,
     tsend,
     trecv,
+    tsend2,
+    trecv2,
+    held,
     rows,
     zrecv,
     local_sem,
     probe_sem,
+    lens_sem,
     frame_sems,
     mask_sems,
     part_sems,
@@ -60,6 +67,8 @@
     ap_r,
     rs_s,
     rs_r,
+    rs2_s,
+    rs2_r,
     rz_s,
     rz_r,
     y_s,
@@ -84,13 +93,6 @@
     def at_z(k):
         return device((z + k) % NZ, x, c, y)
 
-    def at_xy(k):
-        return (x + k // NY) % NX, (y + k % NY) % NY
-
-    def dev_xy(k):
-        px, py = at_xy(k)
-        return device(z, px, c, py)
-
     def at_xyc(k):
         return (x + k // (NY * NC)) % NX, (y + (k // NC) % NY) % NY, (c + k % NC) % NC
 
@@ -113,6 +115,8 @@
         probes.at[pl.ds(pl.multiple_of(y * PIECE, PIECE), PIECE)], pb.at[x, z, y], probe_sem
     )
     mine.start()
+    spans = pltpu.make_async_copy(lengths, lens, lens_sem)
+    spans.start()
     lax.fori_loop(0, NZ * NX, own, 0)
 
     barrier = pltpu.get_barrier_semaphore()
@@ -128,6 +132,7 @@
     lax.fori_loop(1, NZ, greet_z, 0)
     lax.fori_loop(1, NXYC, greet_xyc, 0)
 
+    spans.wait()
     position = lax.broadcasted_iota(jnp.int32, (count, BLOCK), 0)
     inside = jnp.zeros((count, BLOCK), jnp.float32)
     start = jnp.int32(0)
@@ -173,54 +178,61 @@
 
     lax.fori_loop(1, NZ, wait_gather_z, 0)
 
-    def gather_xy(k):
-        return remote(pb.at[x, :, y], pb.at[x, :, y], ap_s.at[k], ap_r.at[k], dev_xy(k))
-
-    def start_gather_xy(k, _):
-        gather_xy(k).start()
-        return 0
-
-    lax.fori_loop(1, NXY, start_gather_xy, 0)
+    def gather_xy(half, dx, dy):
+        if half == 0:
+            px, py = x, (y - dy + NY) % NY if dx else y
+            where = device(z, (x + dx) % NX, c, y) if dx else device(z, x, c, (y + dy) % NY)
+        else:
+            px, py = (x - dx + NX) % NX if dy else x, y
+            where = device(z, x, c, (y + dy) % NY) if dy else device(z, (x + dx) % NX, c, y)
+        piece = pb.at[px, half * HALF : (half + 1) * HALF, py]
+        return remote(piece, piece, ap_s.at[half, dx, dy], ap_r.at[half, dx, dy], where)
+
+    for d in ORDER:
+        gather_xy(0, 0, d).start()
+        gather_xy(1, d, 0).start()
+    for d in ORDER:
+        gather_xy(0, d, 0).start()
+        gather_xy(1, 0, d).start()
+
+    def turn(i, _):
+        block = w[:, pl.ds(pl.multiple_of(i * BLOCK, BLOCK), BLOCK)]
+        wt[i // NZ, i % NZ] = block.T.reshape(NY, PIECE, 2 * count)
+        return 0
 
     mine_rows = w.at[pl.ds(pl.multiple_of(c * count, 128), count)]
     pltpu.make_async_copy(mine_rows, mine_rows, local_sem).wait()
     frames_copy = remote(mine_rows, mine_rows, frame_sems.at[0], frame_sems.at[1], partner)
+
+    for d in ORDER:
+        gather_xy(0, 0, d).wait_recv()
+        for e in ORDER:
+            gather_xy(0, e, d).start()
+        gather_xy(1, d, 0).wait_recv()
+        for e in ORDER:
+            gather_xy(1, d, e).start()
     frames_copy.wait()
     mask_copy.wait()
-
-    def turn(i, _):
-        block = w[:, pl.ds(pl.multiple_of(i * BLOCK, BLOCK), BLOCK)]
-        wt[i // NZ, i % NZ] = block.T.reshape(NY, PIECE, 2 * count)
-        return 0
-
     lax.fori_loop(0, NZ * NX, turn, 0)
 
-    def project(dx, _):
-        def arrived(dy, _):
-            gather_xy(dx * NY + dy).wait_recv()
-            return 0
-
-        lax.fori_loop(jnp.where(dx == 0, 1, 0), NY, arrived, 0)
+    depth = NZ * BLOCK
+    for dx in (0,) + ORDER:
+        for dy in ORDER:
+            if dx:
+                gather_xy(0, dx, dy).wait_recv()
+            gather_xy(1, dx, dy).wait_recv()
+        if dx:
+            gather_xy(0, dx, 0).wait_recv()
         px = (x - dx + NX) % NX
-        depth = NZ * BLOCK
-        block = pb[px].reshape(depth, pb.shape[-1])
         product = jnp.dot(
             w[:, pl.ds(pl.multiple_of(px * depth, depth), depth)],
-            block,
+            pb[px].reshape(depth, pb.shape[-1]),
             preferred_element_type=jnp.float32,
         )
-
-        @pl.when(dx == 0)
-        def _():
+        if dx == 0:
             part[...] = product
-
-        @pl.when(dx > 0)
-        def _():
+        else:
             part[...] += product
-
-        return 0
-
-    lax.fori_loop(0, NX, project, 0)
 
     swap = remote(part, other, part_sems.at[0], part_sems.at[1], partner)
     swap.start()
@@ -230,28 +242,55 @@
     mask = jnp.concatenate([mask, mask], axis=1)
     paired[...] = jnp.where(mask > 0.5, shifted, 0.0).astype(jnp.bfloat16)
 
-    def term(px, py):
-        lhs = wt[px, :, py].reshape(NZ * PIECE, 2 * count)
-        return jnp.dot(lhs, paired[...], preferred_element_type=jnp.float32)
-
-    def scatter_xy(k):
-        return remote(tsend.at[k], trecv.at[k], rs_s.at[k], rs_r.at[k], dev_xy(k))
-
-    def start_scatter_xy(k, _):
-        px, py = at_xy(k)
-        tsend[k] = term(px, py).astype(jnp.bfloat16)
-        scatter_xy(k).start()
-        return 0
-
-    lax.fori_loop(1, NXY, start_scatter_xy, 0)
-    rows[...] = term(x, y)
-
-    def sum_xy(k, _):
-        scatter_xy(k).wait_recv()
-        rows[...] += trecv[k].astype(jnp.float32)
-        return 0
-
-    lax.fori_loop(1, NXY, sum_xy, 0)
+    side = HALF * PIECE
+
+    def scatter_1(half, dx, dy):
+        where = device(z, x, c, (y + dy) % NY) if half else device(z, (x + dx) % NX, c, y)
+        return remote(
+            tsend.at[half, dx, dy],
+            trecv.at[half, dx, dy],
+            rs_s.at[half, dx, dy],
+            rs_r.at[half, dx, dy],
+            where,
+        )
+
+    def scatter_2(half, d):
+        where = device(z, (x + d) % NX, c, y) if half else device(z, x, c, (y + d) % NY)
+        return remote(
+            tsend2.at[half, d], trecv2.at[half, d], rs2_s.at[half, d], rs2_r.at[half, d], where
+        )
+
+    both = [(dx, dy) for dx in ORDER for dy in ORDER]
+    both += [(d, 0) for d in ORDER] + [(0, d) for d in ORDER] + [(0, 0)]
+    for dx, dy in both:
+        lhs = wt[(x + dx) % NX, :, (y + dy) % NY].reshape(NZ * PIECE, 2 * count)
+        term = jnp.dot(lhs, paired[...], preferred_element_type=jnp.float32)
+        for half, away, along in ((0, dx, dy), (1, dy, dx)):
+            mine_term = term[half * side : (half + 1) * side]
+            if away:
+                tsend[half, dx, dy] = mine_term.astype(jnp.bfloat16)
+                scatter_1(half, dx, dy).start()
+            else:
+                held[half, along] = mine_term
+
+    def summed(half, along):
+        total = held[half, along]
+        for d in ORDER:
+            at = (along, d) if half else (d, along)
+            scatter_1(half, *at).wait_recv()
+            total = total + trecv[half, at[0], at[1]].astype(jnp.float32)
+        return total
+
+    for d in ORDER:
+        for half in range(2):
+            tsend2[half, d] = summed(half, d).astype(jnp.bfloat16)
+            scatter_2(half, d).start()
+    for half in range(2):
+        total = summed(half, 0)
+        for d in ORDER:
+            scatter_2(half, d).wait_recv()
+            total = total + trecv2[half, d].astype(jnp.float32)
+        rows[half * side : (half + 1) * side] = total
 
     def scatter_z(k):
         there = (z + k) % NZ
@@ -347,11 +386,6 @@
 
     lax.fori_loop(1, NXYC, start_gather_g, 0)
 
-    def end_xy(k, _):
-        gather_xy(k).wait_send()
-        scatter_xy(k).wait_send()
-        return 0
-
     def end_z(k, _):
         scatter_z(k).wait_send()
         return 0
@@ -364,7 +398,15 @@
         gather_y(k).wait()
         return 0
 
-    lax.fori_loop(1, NXY, end_xy, 0)
+    for half in range(2):
+        for dx in range(NX):
+            for dy in range(NY):
+                if dx or dy:
+                    gather_xy(half, dx, dy).wait_send()
+                if (dy if half else dx):
+                    scatter_1(half, dx, dy).wait_send()
+        for d in ORDER:
+            scatter_2(half, d).wait_send()
     lax.fori_loop(1, NZ, end_z, 0)
     lax.fori_loop(1, NXYC, end_g, 0)
     lax.fori_loop(1, NY, end_y, 0)
@@ -385,12 +427,13 @@
             jax.ShapeDtypeStruct((NXYC, columns // NXYC, columns), f32),
         ),
         in_specs=[
-            pl.BlockSpec(memory_space=pltpu.SMEM),
-            pl.BlockSpec(memory_space=pl.ANY),
-            pl.BlockSpec(memory_space=pl.ANY),
+            pl.BlockSpec(memory_space=pltpu.HBM),
+            pl.BlockSpec(memory_space=pltpu.HBM),
+            pl.BlockSpec(memory_space=pltpu.HBM),
         ],
         out_specs=(pl.BlockSpec(memory_space=pltpu.VMEM), pl.BlockSpec(memory_space=pltpu.VMEM)),
         scratch_shapes=[
+            pltpu.SMEM((1, 1, 4), jnp.int32),
             pltpu.VMEM((NC * count, half), bf16),
             pltpu.VMEM((NX, NZ, NY, PIECE, NC * count), bf16),
             pltpu.VMEM((NX, NZ, NY, PIECE, columns), bf16),
@@ -398,10 +441,14 @@
             pltpu.VMEM((NC * count, columns), f32),
             pltpu.VMEM((NC * count, columns), f32),
             pltpu.VMEM((NC * count, columns), bf16),
-            pltpu.VMEM((NXY, NZ * PIECE, columns), bf16),
-            pltpu.VMEM((NXY, NZ * PIECE, columns), bf16),
+            pltpu.VMEM((2, NX, NY, HALF * PIECE, columns), bf16),
+            pltpu.VMEM((2, NX, NY, HALF * PIECE, columns), bf16),
+            pltpu.VMEM((2, NX, HALF * PIECE, columns), bf16),
+            pltpu.VMEM((2, NX, HALF * PIECE, columns), bf16),
+            pltpu.VMEM((2, NX, HALF * PIECE, columns), f32),
             pltpu.VMEM((NZ * PIECE, columns), f32),
             pltpu.VMEM((NZ, PIECE, columns), f32),
+            dma,
             dma,
             dma,
             dma((2,)),
@@ -409,10 +456,12 @@
             dma((2,)),
             dma((NZ,)),
             dma((NZ,)),
-            dma((NXY,)),
-            dma((NXY,)),
-            dma((NXY,)),
-            dma((NXY,)),
+            dma((2, NX, NY)),
+            dma((2, NX, NY)),
+            dma((2, NX, NY)),
+            dma((2, NX, NY)),
+            dma((2, NX)),
+            dma((2, NX)),
             dma((NZ,)),
             dma((NZ,)),
             dma((NY,)),
@@ -546,6 +595,8 @@
     width = local.shape[1]
     columns = probes.shape[1]
     devices = lax.axis_size("dp") * lax.axis_size("group")
+    lengths = pltpu.with_memory_space_constraint(lengths, pltpu.HBM)
+    probes = pltpu.with_memory_space_constraint(probes, pltpu.HBM)
     sketch, gram = sketch_and_gram(local, lengths, probes, devices)
     gram = gram.reshape(columns, columns)
     return finish(sketch, gram, math.sqrt(width))

time: 127 us -> 98.1 us (0.77)
  Pallas kernels: 125 us -> 97.4 us
  local copies, waits for them, and re-layouts: 1.49 us -> 0 us
    pallas_call x1, Pallas kernels: 113 us -> 85.3 us  [sketch_and_gram(): pl.pallas_call(functools.partial(kernel, scale), out_shape=(jax.ShapeDtyp...]
    unnamed x4 -> x0, local copies, waits for them, and re-layouts: 1.49 us -> none
where the time goes in v3:
time: 98.1 us; the launch traced here: 98 us
  Pallas kernels  97.4 us (99%)
    pallas_call x1, Pallas kernels, sketch_and_gram(): pl.pallas_call(functools.partial(kernel, scale), out_shape=(jax.ShapeDtyp...  85.3 us
    pallas_call x1, Pallas kernels, finish(): pl.pallas_call(functools.partial(finish_kernel, scale), out_shape=(jax.Sh...  12.1 us

profile of v3, /device:TPU:1, one launch (start us, length us, event | category | flops | bytes accessed | tf_op | source)
XLA Modules:
  0.0 98.0 jit_solution(11606819393900245014)
XLA Ops:
  0.6 85.3 %shard_map.50 = (f32[128,256]{1,0:T(8,128)S(1)}, f32[32,8,256]{2,1,0:T(8,128)S(1)}) custom-call(s32[1,1,4]{2,1,0:T(1,128)} %lengths.1, bf16[384,8192]{1,0:T(8,128)(2,1)} %bitcast.3, bf16[128,256]{1,0:T(8,128)(2,1)} %probes.1), custom_call_target="tpu_custom_call" | custom-call | tf_op jit(solution)/shard_map/pallas_call | solution.py:423
  86.0 12.1 %shard_map.51 = (f32[128,256]{1,0:T(8,128)}, f32[256,256]{1,0:T(8,128)}) custom-call(f32[128,256]{1,0:T(8,128)S(1)} %get-tuple-element.4.sketch, f32[256,256]{1,0:T(8,128)S(1)} %bitcast.2), custom_call_target="tpu_custom_call" | custom-call | tf_op jit(solution)/shard_map/pallas_call | solution.py:580

commit v4 on v3

--- a/solution.py
+++ b/solution.py
@@ -1,4 +1,5 @@
 import functools
+import itertools
 import math
 
 import jax
@@ -16,6 +17,12 @@
 PIECE = BLOCK // NY
 HALF = NZ // 2
 ORDER = (1, 3, 2)
+Z_ORDER = (4, 3, 5, 2, 6, 1, 7)
+XYC_ORDER = sorted(
+    (k for k in itertools.product(range(NX), range(NY), range(NC)) if any(k)),
+    key=lambda k: -min(k[0], NX - k[0]) - min(k[1], NY - k[1]),
+)
+TURNS = (14, 18, 26)
 
 
 def device(z, x, c, y):
@@ -90,17 +97,29 @@
     z = dp // (NC * NX)
     count = frames.shape[0]
 
+    xs = [x] + [(x + d) % NX for d in range(1, NX)]
+    ys = [y] + [(y + d) % NY for d in range(1, NY)]
+    cs = [c, 1 - c]
+    zs = [z] + [(z + d) % NZ for d in range(1, NZ)]
+
     def at_z(k):
-        return device((z + k) % NZ, x, c, y)
+        return device(zs[k], x, c, y)
+
+    def place(k):
+        dx, dy, dc = k
+        return (xs[dx] * NY + ys[dy]) * NC + cs[dc]
 
     def at_xyc(k):
-        return (x + k // (NY * NC)) % NX, (y + (k // NC) % NY) % NY, (c + k % NC) % NC
-
-    def dev_xyc(k):
-        px, py, pc = at_xyc(k)
-        return device(z, px, pc, py)
+        dx, dy, dc = k
+        return device(z, xs[dx], cs[dc], ys[dy])
 
     partner = device(z, x, 1 - c, y)
+
+    barrier = pltpu.get_barrier_semaphore()
+    for k in XYC_ORDER:
+        pl.semaphore_signal(barrier, inc=1, device_id=at_xyc(k), device_id_type=MESH)
+    for k in Z_ORDER:
+        pl.semaphore_signal(barrier, inc=1, device_id=at_z(k), device_id_type=MESH)
 
     def own(i, _):
         col = ((i % NZ) * NX + i // NZ) * NC + c
@@ -118,19 +137,6 @@
     spans = pltpu.make_async_copy(lengths, lens, lens_sem)
     spans.start()
     lax.fori_loop(0, NZ * NX, own, 0)
-
-    barrier = pltpu.get_barrier_semaphore()
-
-    def greet_z(k, _):
-        pl.semaphore_signal(barrier, inc=1, device_id=at_z(k), device_id_type=MESH)
-        return 0
-
-    def greet_xyc(k, _):
-        pl.semaphore_signal(barrier, inc=1, device_id=dev_xyc(k), device_id_type=MESH)
-        return 0
-
-    lax.fori_loop(1, NZ, greet_z, 0)
-    lax.fori_loop(1, NXYC, greet_xyc, 0)
 
     spans.wait()
     position = lax.broadcasted_iota(jnp.int32, (count, BLOCK), 0)
@@ -151,11 +157,8 @@
     def gather_z(k):
         return remote(pb.at[x, z, y], pb.at[x, z, y], az_s.at[k], az_r.at[k], at_z(k))
 
-    def start_gather_z(k, _):
+    for k in Z_ORDER:
         gather_z(k).start()
-        return 0
-
-    lax.fori_loop(1, NZ, start_gather_z, 0)
 
     def give(i, _):
         col = ((i % NZ) * NX + i // NZ) * NC + (1 - c)
@@ -172,11 +175,8 @@
     mask_copy = remote(masks.at[c], masks.at[c], mask_sems.at[0], mask_sems.at[1], partner)
     mask_copy.start()
 
-    def wait_gather_z(k, _):
-        gather_z(k).wait()
-        return 0
-
-    lax.fori_loop(1, NZ, wait_gather_z, 0)
+    for k in Z_ORDER:
+        gather_z(k).wait_recv()
 
     def gather_xy(half, dx, dy):
         if half == 0:
@@ -196,24 +196,36 @@
         gather_xy(1, 0, d).start()
 
     def turn(i, _):
-        block = w[:, pl.ds(pl.multiple_of(i * BLOCK, BLOCK), BLOCK)]
+        at = pl.ds(pl.multiple_of(i * BLOCK, BLOCK), BLOCK)
+        block = w[:, at]
         wt[i // NZ, i % NZ] = block.T.reshape(NY, PIECE, 2 * count)
+        moved = pltpu.roll(block.astype(jnp.float32), 1, 0)
+        keep = masks[...].reshape(2 * count, BLOCK) > 0.5
+        w[:, at] = jnp.where(keep, moved, 0.0).astype(jnp.bfloat16)
         return 0
 
     mine_rows = w.at[pl.ds(pl.multiple_of(c * count, 128), count)]
     pltpu.make_async_copy(mine_rows, mine_rows, local_sem).wait()
     frames_copy = remote(mine_rows, mine_rows, frame_sems.at[0], frame_sems.at[1], partner)
-
-    for d in ORDER:
+    frames_copy.wait()
+    mask_copy.wait()
+
+    turned = 0
+    for d, until in zip(ORDER, TURNS):
+        lax.fori_loop(turned, until, turn, 0)
+        turned = until
         gather_xy(0, 0, d).wait_recv()
         for e in ORDER:
             gather_xy(0, e, d).start()
         gather_xy(1, d, 0).wait_recv()
         for e in ORDER:
             gather_xy(1, d, e).start()
-    frames_copy.wait()
-    mask_copy.wait()
-    lax.fori_loop(0, NZ * NX, turn, 0)
+    lax.fori_loop(turned, NZ * NX, turn, 0)
+
+    def swap(core):
+        return remote(
+            part.at[core], other.at[core], part_sems.at[0, core], part_sems.at[1, core], partner
+        )
 
     depth = NZ * BLOCK
     for dx in (0,) + ORDER:
@@ -224,23 +236,23 @@
         if dx:
             gather_xy(0, dx, 0).wait_recv()
         px = (x - dx + NX) % NX
-        product = jnp.dot(
-            w[:, pl.ds(pl.multiple_of(px * depth, depth), depth)],
-            pb[px].reshape(depth, pb.shape[-1]),
-            preferred_element_type=jnp.float32,
-        )
-        if dx == 0:
-            part[...] = product
-        else:
-            part[...] += product
-
-    swap = remote(part, other, part_sems.at[0], part_sems.at[1], partner)
-    swap.start()
-    swap.wait()
-    shifted = pltpu.roll(part[...] + other[...], 1, 0)
-    mask = masks[...].reshape(2 * count, BLOCK)
-    mask = jnp.concatenate([mask, mask], axis=1)
-    paired[...] = jnp.where(mask > 0.5, shifted, 0.0).astype(jnp.bfloat16)
+        block = pb[px].reshape(depth, pb.shape[-1])
+        for core in range(NC):
+            its = slice(core * count, (core + 1) * count)
+            product = jnp.dot(
+                w[its, pl.ds(pl.multiple_of(px * depth, depth), depth)],
+                block,
+                preferred_element_type=jnp.float32,
+            )
+            if dx == 0:
+                part[core] = product
+            else:
+                part[core] += product
+            if dx == ORDER[-1]:
+                swap(core).start()
+    for core in range(NC):
+        swap(core).wait()
+        paired[core * count : (core + 1) * count] = (part[core] + other[core]).astype(jnp.bfloat16)
 
     side = HALF * PIECE
 
@@ -293,7 +305,7 @@
         rows[half * side : (half + 1) * side] = total
 
     def scatter_z(k):
-        there = (z + k) % NZ
+        there = zs[k]
         return remote(
             rows.at[pl.ds(pl.multiple_of(there * PIECE, PIECE), PIECE)],
             zrecv.at[k],
@@ -302,18 +314,13 @@
             at_z(k),
         )
 
-    def start_scatter_z(k, _):
+    for k in Z_ORDER:
         scatter_z(k).start()
-        return 0
-
-    lax.fori_loop(1, NZ, start_scatter_z, 0)
     total = rows[pl.ds(pl.multiple_of(z * PIECE, PIECE), PIECE)]
-
-    def sum_z(k, total):
+    for k in reversed(Z_ORDER):
         scatter_z(k).wait_recv()
-        return total + zrecv[k]
-
-    total = lax.fori_loop(1, NZ, sum_z, total) * scale
+        total = total + zrecv[k]
+    total = total * scale
     here = pl.ds(pl.multiple_of(y * PIECE, PIECE), PIECE)
     sketch_ref[here] = total
 
@@ -323,7 +330,7 @@
             sketch_ref.at[here],
             y_s.at[k],
             y_r.at[k],
-            device(z, x, c, (y + k) % NY),
+            device(z, x, c, ys[k]),
         )
 
     gsend[...] = jnp.dot(
@@ -331,72 +338,38 @@
     ).reshape(gsend.shape)
 
     def scatter_g(k):
-        px, py, pc = at_xyc(k)
-        return remote(
-            gsend.at[(px * NY + py) * NC + pc], grecv.at[k], g_s.at[k], g_r.at[k], dev_xyc(k)
-        )
-
-    def start_scatter_g(k, _):
+        i = XYC_ORDER.index(k)
+        return remote(gsend.at[place(k)], grecv.at[i], g_s.at[i], g_r.at[i], at_xyc(k))
+
+    for k in XYC_ORDER:
         scatter_g(k).start()
-        return 0
-
-    lax.fori_loop(1, NXYC, start_scatter_g, 0)
-
-    def start_gather_y(k, _):
-        gather_y(k).start()
-        return 0
-
-    lax.fori_loop(1, NY, start_gather_y, 0)
-    me = (x * NY + y) * NC + c
-
-    def sum_g(k, acc):
+    me = place((0, 0, 0))
+    acc = gsend[me]
+    for k in reversed(XYC_ORDER):
         scatter_g(k).wait_recv()
-        return acc + grecv[k]
-
-    gz[z] = lax.fori_loop(1, NXYC, sum_g, gsend[me])
+        acc = acc + grecv[XYC_ORDER.index(k)]
+    gz[z] = acc
 
     def spread_z(k):
         return remote(gz.at[z], gz.at[z], gz_s.at[k], gz_r.at[k], at_z(k))
 
-    def start_spread_z(k, _):
+    for k in Z_ORDER:
         spread_z(k).start()
-        return 0
-
-    def wait_spread_z(k, _):
-        spread_z(k).wait()
-        return 0
-
-    lax.fori_loop(1, NZ, start_spread_z, 0)
-    lax.fori_loop(1, NZ, wait_spread_z, 0)
+    for k in ORDER:
+        gather_y(k).start()
+    for k in Z_ORDER:
+        spread_z(k).wait_recv()
     acc = gz[0]
     for k in range(1, NZ):
         acc = acc + gz[k]
     gram_ref[me] = acc
 
     def gather_g(k):
-        return remote(gram_ref.at[me], gram_ref.at[me], ga_s.at[k], ga_r.at[k], dev_xyc(k))
-
-    def start_gather_g(k, _):
+        i = XYC_ORDER.index(k)
+        return remote(gram_ref.at[me], gram_ref.at[me], ga_s.at[i], ga_r.at[i], at_xyc(k))
+
+    for k in XYC_ORDER:
         gather_g(k).start()
-        return 0
-
-    def wait_gather_g(k, _):
-        gather_g(k).wait()
-        return 0
-
-    lax.fori_loop(1, NXYC, start_gather_g, 0)
-
-    def end_z(k, _):
-        scatter_z(k).wait_send()
-        return 0
-
-    def end_g(k, _):
-        scatter_g(k).wait_send()
-        return 0
-
-    def end_y(k, _):
-        gather_y(k).wait()
-        return 0
 
     for half in range(2):
         for dx in range(NX):
@@ -407,10 +380,16 @@
                     scatter_1(half, dx, dy).wait_send()
         for d in ORDER:
             scatter_2(half, d).wait_send()
-    lax.fori_loop(1, NZ, end_z, 0)
-    lax.fori_loop(1, NXYC, end_g, 0)
-    lax.fori_loop(1, NY, end_y, 0)
-    lax.fori_loop(1, NXYC, wait_gather_g, 0)
+    for k in Z_ORDER:
+        gather_z(k).wait_send()
+        scatter_z(k).wait_send()
+        spread_z(k).wait_send()
+    for k in XYC_ORDER:
+        scatter_g(k).wait_send()
+    for k in ORDER:
+        gather_y(k).wait()
+    for k in reversed(XYC_ORDER):
+        gather_g(k).wait()
 
 
 def sketch_and_gram(frames, lengths, probes, devices):
@@ -438,8 +417,8 @@
             pltpu.VMEM((NX, NZ, NY, PIECE, NC * count), bf16),
             pltpu.VMEM((NX, NZ, NY, PIECE, columns), bf16),
             pltpu.VMEM((NC, count, BLOCK), f32),
-            pltpu.VMEM((NC * count, columns), f32),
-            pltpu.VMEM((NC * count, columns), f32),
+            pltpu.VMEM((NC, count, columns), f32),
+            pltpu.VMEM((NC, count, columns), f32),
             pltpu.VMEM((NC * count, columns), bf16),
             pltpu.VMEM((2, NX, NY, HALF * PIECE, columns), bf16),
             pltpu.VMEM((2, NX, NY, HALF * PIECE, columns), bf16),
@@ -453,7 +432,7 @@
             dma,
             dma((2,)),
             dma((2,)),
-            dma((2,)),
+            dma((2, NC)),
             dma((NZ,)),
             dma((NZ,)),
             dma((2, NX, NY)),
@@ -514,11 +493,7 @@
         first = top // LANES
         tiles = [(a, t) for t in range(first, lane_tiles)] + [(b, t) for t in range(first + 1)]
         many = range(len(tiles))
-        columns = [
-            splat(a[top : top + PANEL, top + j : top + j + 1])
-            for j in range(PANEL)
-        ]
-        d = [[splat(lax.slice(columns[j], (i, 0), (i + 1, LANES))) for j in range(i + 1)] for i in range(PANEL)]
+        d = [[splat(a[top + i : top + i + 1, top + j : top + j + 1]) for j in range(i + 1)] for i in range(PANEL)]
         rows = [[splat(tile(ref, top + i, 1, t)[...]) for ref, t in tiles] for i in range(PANEL)]
         m = [[None] * PANEL for _ in range(PANEL)]
         inv = [None] * PANEL
@@ -551,8 +526,9 @@
                 block[...] = value
             return 0
 
-        if p + 1 < panels:
-            lax.fori_loop(p + 1, panels, update, 0, unroll=True)
+        last = (first + 1) * LANES // PANEL
+        if p + 1 < last:
+            lax.fori_loop(p + 1, last, update, 0, unroll=True)
         for i in range(PANEL):
             root = lax.rsqrt(d[i][i])
             for t in range(lane_tiles):
@@ -567,6 +543,18 @@
                     lower = (rows[i][lane_tiles - first + t] * root)[0:1]
                 tile(factor, top + i, 1, t)[...] = upper
                 tile(inverse, top + i, 1, t)[...] = lower
+        if p + 1 == last and last < panels:
+            done, below = top + PANEL - LANES, top + PANEL
+            right = factor[done:below, below:]
+            taken = lax.dot_general(
+                right,
+                jnp.concatenate([inverse[done:below, :below], right], axis=1),
+                (((0,), (0,)), ((), ())),
+                precision=lax.Precision.HIGHEST,
+                preferred_element_type=jnp.float32,
+            )
+            b[below:, :below] = b[below:, :below] - taken[:, :below]
+            a[below:, below:] = a[below:, below:] - taken[:, below:]
     basis[...] = scale * lax.dot_general(
         sketch[...],
         inverse[...],

time: 98.1 us -> 88.7 us (0.904)
  Pallas kernels: 97.4 us -> 88 us
    pallas_call x1, Pallas kernels: 85.3 us -> 79.5 us  [sketch_and_gram(): pl.pallas_call(functools.partial(kernel, scale), out_shape=(jax.ShapeDtyp...]
    pallas_call x1, Pallas kernels: 12.1 us -> 8.46 us  [finish(): pl.pallas_call(functools.partial(finish_kernel, scale), out_shape=(jax.Sh...]
where the time goes in v4:
time: 88.7 us; the launch traced here: 88.6 us
  Pallas kernels  88 us (99%)
    pallas_call x1, Pallas kernels, sketch_and_gram(): pl.pallas_call(functools.partial(kernel, scale), out_shape=(jax.ShapeDtyp...  79.5 us
    pallas_call x1, Pallas kernels, finish(): pl.pallas_call(functools.partial(finish_kernel, scale), out_shape=(jax.Sh...  8.46 us

profile of v4, /device:TPU:1, one launch (start us, length us, event | category | flops | bytes accessed | tf_op | source)
XLA Modules:
  0.0 88.6 jit_solution(3497760272479427626)
XLA Ops:
  0.6 79.5 %shard_map.50 = (f32[128,256]{1,0:T(8,128)S(1)}, f32[32,8,256]{2,1,0:T(8,128)S(1)}) custom-call(s32[1,1,4]{2,1,0:T(1,128)} %lengths.1, bf16[384,8192]{1,0:T(8,128)(2,1)} %bitcast.3, bf16[128,256]{1,0:T(8,128)(2,1)} %probes.1), custom_call_target="tpu_custom_call" | custom-call | tf_op jit(solution)/shard_map/pallas_call | solution.py:402
  80.1 8.5 %shard_map.51 = (f32[128,256]{1,0:T(8,128)}, f32[256,256]{1,0:T(8,128)}) custom-call(f32[128,256]{1,0:T(8,128)S(1)} %get-tuple-element.4.sketch, f32[256,256]{1,0:T(8,128)S(1)} %bitcast.2), custom_call_target="tpu_custom_call" | custom-call | tf_op jit(solution)/shard_map/pallas_call | solution.py:568

commit v5 on v4

--- a/solution.py
+++ b/solution.py
@@ -15,14 +15,17 @@
 NXYC = NXY * NC
 BLOCK = 128
 PIECE = BLOCK // NY
-HALF = NZ // 2
+PAIR = 2
+GROUPS = NZ // PAIR
 ORDER = (1, 3, 2)
+REL = (0, 1, 7, 2, 6, 3, 5, 4)
+SLOT = tuple(REL.index(k) for k in range(NZ))
 Z_ORDER = (4, 3, 5, 2, 6, 1, 7)
 XYC_ORDER = sorted(
     (k for k in itertools.product(range(NX), range(NY), range(NC)) if any(k)),
     key=lambda k: -min(k[0], NX - k[0]) - min(k[1], NY - k[1]),
 )
-TURNS = (14, 18, 26)
+TURNS = (18, 22, 27)
 
 
 def device(z, x, c, y):
@@ -121,22 +124,28 @@
     for k in Z_ORDER:
         pl.semaphore_signal(barrier, inc=1, device_id=at_z(k), device_id_type=MESH)
 
-    def own(i, _):
-        col = ((i % NZ) * NX + i // NZ) * NC + c
-        pltpu.make_async_copy(
-            frames.at[:, pl.ds(pl.multiple_of(col * BLOCK, BLOCK), BLOCK)],
-            w.at[pl.ds(pl.multiple_of(c * count, 128), count), pl.ds(pl.multiple_of(i * BLOCK, BLOCK), BLOCK)],
-            local_sem,
-        ).start()
-        return 0
+    def columns_of(s, i, core):
+        return pl.ds(pl.multiple_of(((zs[-REL[s]] * NX + i) * NC + core) * BLOCK, BLOCK), BLOCK)
+
+    def places_of(s, i):
+        at = pl.ds(pl.multiple_of((i * NZ + s) * BLOCK, BLOCK), BLOCK)
+        return w.at[pl.ds(pl.multiple_of(c * count, 128), count), at]
 
     mine = pltpu.make_async_copy(
-        probes.at[pl.ds(pl.multiple_of(y * PIECE, PIECE), PIECE)], pb.at[x, z, y], probe_sem
+        probes.at[pl.ds(pl.multiple_of(y * PIECE, PIECE), PIECE)], pb.at[x, 0, y], probe_sem
     )
     mine.start()
     spans = pltpu.make_async_copy(lengths, lens, lens_sem)
     spans.start()
-    lax.fori_loop(0, NZ * NX, own, 0)
+    for s in range(NZ):
+
+        def own(i, _, s=s):
+            pltpu.make_async_copy(
+                frames.at[:, columns_of(s, i, c)], places_of(s, i), local_sem
+            ).start()
+            return 0
+
+        lax.fori_loop(0, NX, own, 0)
 
     spans.wait()
     position = lax.broadcasted_iota(jnp.int32, (count, BLOCK), 0)
@@ -155,45 +164,47 @@
     mine.wait()
 
     def gather_z(k):
-        return remote(pb.at[x, z, y], pb.at[x, z, y], az_s.at[k], az_r.at[k], at_z(k))
-
-    for k in Z_ORDER:
+        return remote(pb.at[x, 0, y], pb.at[x, SLOT[k], y], az_s.at[k], az_r.at[k], at_z(k))
+
+    for k in REL[1:]:
         gather_z(k).start()
 
-    def give(i, _):
-        col = ((i % NZ) * NX + i // NZ) * NC + (1 - c)
-        remote(
-            frames.at[:, pl.ds(pl.multiple_of(col * BLOCK, BLOCK), BLOCK)],
-            w.at[pl.ds(pl.multiple_of(c * count, 128), count), pl.ds(pl.multiple_of(i * BLOCK, BLOCK), BLOCK)],
-            frame_sems.at[0],
-            frame_sems.at[1],
-            partner,
-        ).start()
-        return 0
-
-    lax.fori_loop(0, NZ * NX, give, 0)
+    for s in range(NZ):
+
+        def give(i, _, s=s):
+            remote(
+                frames.at[:, columns_of(s, i, 1 - c)],
+                places_of(s, i),
+                frame_sems.at[0],
+                frame_sems.at[1],
+                partner,
+            ).start()
+            return 0
+
+        lax.fori_loop(0, NX, give, 0)
     mask_copy = remote(masks.at[c], masks.at[c], mask_sems.at[0], mask_sems.at[1], partner)
     mask_copy.start()
 
-    for k in Z_ORDER:
-        gather_z(k).wait_recv()
-
-    def gather_xy(half, dx, dy):
-        if half == 0:
-            px, py = x, (y - dy + NY) % NY if dx else y
-            where = device(z, (x + dx) % NX, c, y) if dx else device(z, x, c, (y + dy) % NY)
+    def gather_xy(group, dx, dy):
+        if group % 2 == 0:
+            px, py = x, ys[-dy] if dx else y
+            where = device(z, xs[dx], c, y) if dx else device(z, x, c, ys[dy])
         else:
-            px, py = (x - dx + NX) % NX if dy else x, y
-            where = device(z, x, c, (y + dy) % NY) if dy else device(z, (x + dx) % NX, c, y)
-        piece = pb.at[px, half * HALF : (half + 1) * HALF, py]
-        return remote(piece, piece, ap_s.at[half, dx, dy], ap_r.at[half, dx, dy], where)
-
-    for d in ORDER:
-        gather_xy(0, 0, d).start()
-        gather_xy(1, d, 0).start()
-    for d in ORDER:
-        gather_xy(0, d, 0).start()
-        gather_xy(1, 0, d).start()
+            px, py = xs[-dx] if dy else x, y
+            where = device(z, x, c, ys[dy]) if dy else device(z, xs[dx], c, y)
+        piece = pb.at[px, group * PAIR : (group + 1) * PAIR, py]
+        return remote(piece, piece, ap_s.at[group, dx, dy], ap_r.at[group, dx, dy], where)
+
+    def leg(group, first, second):
+        return gather_xy(group, *((second, first) if group % 2 == 0 else (first, second)))
+
+    for group in range(GROUPS):
+        for slot in range(max(1, group * PAIR), (group + 1) * PAIR):
+            gather_z(REL[slot]).wait_recv()
+        for d in ORDER:
+            leg(group, d, 0).start()
+        for d in ORDER:
+            leg(group, 0, d).start()
 
     def turn(i, _):
         at = pl.ds(pl.multiple_of(i * BLOCK, BLOCK), BLOCK)
@@ -204,22 +215,25 @@
         w[:, at] = jnp.where(keep, moved, 0.0).astype(jnp.bfloat16)
         return 0
 
+    def forward(group, d):
+        leg(group, d, 0).wait_recv()
+        for e in ORDER:
+            leg(group, d, e).start()
+
+    for d in ORDER:
+        forward(0, d)
+        forward(1, d)
     mine_rows = w.at[pl.ds(pl.multiple_of(c * count, 128), count)]
     pltpu.make_async_copy(mine_rows, mine_rows, local_sem).wait()
     frames_copy = remote(mine_rows, mine_rows, frame_sems.at[0], frame_sems.at[1], partner)
     frames_copy.wait()
     mask_copy.wait()
-
     turned = 0
     for d, until in zip(ORDER, TURNS):
         lax.fori_loop(turned, until, turn, 0)
         turned = until
-        gather_xy(0, 0, d).wait_recv()
-        for e in ORDER:
-            gather_xy(0, e, d).start()
-        gather_xy(1, d, 0).wait_recv()
-        for e in ORDER:
-            gather_xy(1, d, e).start()
+        forward(2, d)
+        forward(3, d)
     lax.fori_loop(turned, NZ * NX, turn, 0)
 
     def swap(core):
@@ -229,13 +243,11 @@
 
     depth = NZ * BLOCK
     for dx in (0,) + ORDER:
-        for dy in ORDER:
-            if dx:
-                gather_xy(0, dx, dy).wait_recv()
-            gather_xy(1, dx, dy).wait_recv()
-        if dx:
-            gather_xy(0, dx, 0).wait_recv()
-        px = (x - dx + NX) % NX
+        for group in range(GROUPS):
+            for dy in range(NY):
+                if (dx if group % 2 == 0 else dy):
+                    gather_xy(group, dx, dy).wait_recv()
+        px = xs[-dx]
         block = pb[px].reshape(depth, pb.shape[-1])
         for core in range(NC):
             its = slice(core * count, (core + 1) * count)
@@ -254,72 +266,74 @@
         swap(core).wait()
         paired[core * count : (core + 1) * count] = (part[core] + other[core]).astype(jnp.bfloat16)
 
-    side = HALF * PIECE
-
-    def scatter_1(half, dx, dy):
-        where = device(z, x, c, (y + dy) % NY) if half else device(z, (x + dx) % NX, c, y)
+    side = PAIR * PIECE
+
+    def scatter_1(group, dx, dy):
+        where = device(z, x, c, ys[dy]) if group % 2 else device(z, xs[dx], c, y)
         return remote(
-            tsend.at[half, dx, dy],
-            trecv.at[half, dx, dy],
-            rs_s.at[half, dx, dy],
-            rs_r.at[half, dx, dy],
+            tsend.at[group, dx, dy],
+            trecv.at[group, dx, dy],
+            rs_s.at[group, dx, dy],
+            rs_r.at[group, dx, dy],
             where,
         )
 
-    def scatter_2(half, d):
-        where = device(z, (x + d) % NX, c, y) if half else device(z, x, c, (y + d) % NY)
+    def scatter_2(group, d):
+        where = device(z, xs[d], c, y) if group % 2 else device(z, x, c, ys[d])
         return remote(
-            tsend2.at[half, d], trecv2.at[half, d], rs2_s.at[half, d], rs2_r.at[half, d], where
+            tsend2.at[group, d], trecv2.at[group, d], rs2_s.at[group, d], rs2_r.at[group, d], where
+        )
+
+    def scatter_z(s):
+        return remote(
+            rows.at[s * PIECE : (s + 1) * PIECE],
+            zrecv.at[s],
+            rz_s.at[s],
+            rz_r.at[s],
+            at_z(NZ - REL[s]),
         )
 
     both = [(dx, dy) for dx in ORDER for dy in ORDER]
     both += [(d, 0) for d in ORDER] + [(0, d) for d in ORDER] + [(0, 0)]
-    for dx, dy in both:
-        lhs = wt[(x + dx) % NX, :, (y + dy) % NY].reshape(NZ * PIECE, 2 * count)
-        term = jnp.dot(lhs, paired[...], preferred_element_type=jnp.float32)
-        for half, away, along in ((0, dx, dy), (1, dy, dx)):
-            mine_term = term[half * side : (half + 1) * side]
-            if away:
-                tsend[half, dx, dy] = mine_term.astype(jnp.bfloat16)
-                scatter_1(half, dx, dy).start()
-            else:
-                held[half, along] = mine_term
-
-    def summed(half, along):
-        total = held[half, along]
+    for groups in ((2, 3), (0, 1)):
+        for dx, dy in both:
+            slots = slice(groups[0] * PAIR, (groups[1] + 1) * PAIR)
+            lhs = wt[xs[dx], slots, ys[dy]].reshape(2 * side, 2 * count)
+            term = jnp.dot(lhs, paired[...], preferred_element_type=jnp.float32)
+            for group, away, along in ((groups[0], dx, dy), (groups[1], dy, dx)):
+                mine_term = term[(group % 2) * side : (group % 2 + 1) * side]
+                if away:
+                    tsend[group, dx, dy] = mine_term.astype(jnp.bfloat16)
+                    scatter_1(group, dx, dy).start()
+                else:
+                    held[group, along] = mine_term
+
+    def summed(group, along):
+        total = held[group, along]
         for d in ORDER:
-            at = (along, d) if half else (d, along)
-            scatter_1(half, *at).wait_recv()
-            total = total + trecv[half, at[0], at[1]].astype(jnp.float32)
+            at = (along, d) if group % 2 else (d, along)
+            scatter_1(group, *at).wait_recv()
+            total = total + trecv[group, at[0], at[1]].astype(jnp.float32)
         return total
 
-    for d in ORDER:
-        for half in range(2):
-            tsend2[half, d] = summed(half, d).astype(jnp.bfloat16)
-            scatter_2(half, d).start()
-    for half in range(2):
-        total = summed(half, 0)
+    for groups in ((2, 3), (0, 1)):
         for d in ORDER:
-            scatter_2(half, d).wait_recv()
-            total = total + trecv2[half, d].astype(jnp.float32)
-        rows[half * side : (half + 1) * side] = total
-
-    def scatter_z(k):
-        there = zs[k]
-        return remote(
-            rows.at[pl.ds(pl.multiple_of(there * PIECE, PIECE), PIECE)],
-            zrecv.at[k],
-            rz_s.at[k],
-            rz_r.at[k],
-            at_z(k),
-        )
-
-    for k in Z_ORDER:
-        scatter_z(k).start()
-    total = rows[pl.ds(pl.multiple_of(z * PIECE, PIECE), PIECE)]
-    for k in reversed(Z_ORDER):
-        scatter_z(k).wait_recv()
-        total = total + zrecv[k]
+            for group in groups:
+                tsend2[group, d] = summed(group, d).astype(jnp.bfloat16)
+                scatter_2(group, d).start()
+        for group in groups:
+            total = summed(group, 0)
+            for d in ORDER:
+                scatter_2(group, d).wait_recv()
+                total = total + trecv2[group, d].astype(jnp.float32)
+            rows[group * side : (group + 1) * side] = total
+            for slot in reversed(range(max(1, group * PAIR), (group + 1) * PAIR)):
+                scatter_z(slot).start()
+
+    total = rows[:PIECE]
+    for slot in reversed(range(1, NZ)):
+        scatter_z(slot).wait_recv()
+        total = total + zrecv[slot]
     total = total * scale
     here = pl.ds(pl.multiple_of(y * PIECE, PIECE), PIECE)
     sketch_ref[here] = total
@@ -371,15 +385,15 @@
     for k in XYC_ORDER:
         gather_g(k).start()
 
-    for half in range(2):
+    for group in range(GROUPS):
         for dx in range(NX):
             for dy in range(NY):
                 if dx or dy:
-                    gather_xy(half, dx, dy).wait_send()
-                if (dy if half else dx):
-                    scatter_1(half, dx, dy).wait_send()
+                    gather_xy(group, dx, dy).wait_send()
+                if (dy if group % 2 else dx):
+                    scatter_1(group, dx, dy).wait_send()
         for d in ORDER:
-            scatter_2(half, d).wait_send()
+            scatter_2(group, d).wait_send()
     for k in Z_ORDER:
         gather_z(k).wait_send()
         scatter_z(k).wait_send()
@@ -420,11 +434,11 @@
             pltpu.VMEM((NC, count, columns), f32),
             pltpu.VMEM((NC, count, columns), f32),
             pltpu.VMEM((NC * count, columns), bf16),
-            pltpu.VMEM((2, NX, NY, HALF * PIECE, columns), bf16),
-            pltpu.VMEM((2, NX, NY, HALF * PIECE, columns), bf16),
-            pltpu.VMEM((2, NX, HALF * PIECE, columns), bf16),
-            pltpu.VMEM((2, NX, HALF * PIECE, columns), bf16),
-            pltpu.VMEM((2, NX, HALF * PIECE, columns), f32),
+            pltpu.VMEM((GROUPS, NX, NY, PAIR * PIECE, columns), bf16),
+            pltpu.VMEM((GROUPS, NX, NY, PAIR * PIECE, columns), bf16),
+            pltpu.VMEM((GROUPS, NX, PAIR * PIECE, columns), bf16),
+            pltpu.VMEM((GROUPS, NX, PAIR * PIECE, columns), bf16),
+            pltpu.VMEM((GROUPS, NX, PAIR * PIECE, columns), f32),
             pltpu.VMEM((NZ * PIECE, columns), f32),
             pltpu.VMEM((NZ, PIECE, columns), f32),
             dma,
@@ -435,12 +449,12 @@
             dma((2, NC)),
             dma((NZ,)),
             dma((NZ,)),
-            dma((2, NX, NY)),
-            dma((2, NX, NY)),
-            dma((2, NX, NY)),
-            dma((2, NX, NY)),
-            dma((2, NX)),
-            dma((2, NX)),
+            dma((GROUPS, NX, NY)),
+            dma((GROUPS, NX, NY)),
+            dma((GROUPS, NX, NY)),
+            dma((GROUPS, NX, NY)),
+            dma((GROUPS, NX)),
+            dma((GROUPS, NX)),
             dma((NZ,)),
             dma((NZ,)),
             dma((NY,)),

time: 88.7 us -> 86.5 us (0.975)
  Pallas kernels: 88 us -> 85.8 us
    pallas_call x1, Pallas kernels: 79.5 us -> 77.3 us  [sketch_and_gram(): pl.pallas_call(functools.partial(kernel, scale), out_shape=(jax.ShapeDtyp...]
where the time goes in v5:
time: 86.5 us; the launch traced here: 86.4 us
  Pallas kernels  85.8 us (99%)
    pallas_call x1, Pallas kernels, sketch_and_gram(): pl.pallas_call(functools.partial(kernel, scale), out_shape=(jax.ShapeDtyp...  77.3 us
    pallas_call x1, Pallas kernels, finish(): pl.pallas_call(functools.partial(finish_kernel, scale), out_shape=(jax.Sh...  8.46 us

profile of v5, /device:TPU:1, one launch (start us, length us, event | category | flops | bytes accessed | tf_op | source)
XLA Modules:
  0.0 86.4 jit_solution(8740179488714045731)
XLA Ops:
  0.6 77.3 %shard_map.50 = (f32[128,256]{1,0:T(8,128)S(1)}, f32[32,8,256]{2,1,0:T(8,128)S(1)}) custom-call(s32[1,1,4]{2,1,0:T(1,128)} %lengths.1, bf16[384,8192]{1,0:T(8,128)(2,1)} %bitcast.3, bf16[128,256]{1,0:T(8,128)(2,1)} %probes.1), custom_call_target="tpu_custom_call" | custom-call | tf_op jit(solution)/shard_map/pallas_call | solution.py:416
  78.0 8.5 %shard_map.51 = (f32[128,256]{1,0:T(8,128)}, f32[256,256]{1,0:T(8,128)}) custom-call(f32[128,256]{1,0:T(8,128)S(1)} %get-tuple-element.4.sketch, f32[256,256]{1,0:T(8,128)S(1)} %bitcast.2), custom_call_target="tpu_custom_call" | custom-call | tf_op jit(solution)/shard_map/pallas_call | solution.py:582

commit v6 on v5

--- a/solution.py
+++ b/solution.py
@@ -487,7 +487,7 @@
     return lax.sub(x, lax.mul(y, z))
 
 
-def finish_kernel(scale, sketch, gram, basis, factor, a, b, inverse):
+def finish_kernel(scale, sketch, gram, basis_out, factor_out, a, b, inverse, factor, basis, sems):
     n = gram.shape[0]
     panels = n // PANEL
     lane_tiles = n // LANES
@@ -497,6 +497,9 @@
         1.0,
         0.0,
     )
+
+    def send(here, there, k):
+        return pltpu.make_async_copy(here, there, sems.at[k])
 
     def tile(ref, top, rows, t):
         return ref.at[top : top + rows, t * LANES : (t + 1) * LANES]
@@ -569,13 +572,20 @@
             )
             b[below:, :below] = b[below:, :below] - taken[:, :below]
             a[below:, below:] = a[below:, below:] - taken[:, below:]
-    basis[...] = scale * lax.dot_general(
-        sketch[...],
-        inverse[...],
-        (((1,), (1,)), ((), ())),
-        precision=lax.Precision.HIGHEST,
-        preferred_element_type=jnp.float32,
-    )
+        if p + 1 == last:
+            send(factor.at[last * PANEL - LANES : last * PANEL], factor_out.at[last * PANEL - LANES : last * PANEL], 2 * first).start()
+            basis[first] = scale * lax.dot_general(
+                sketch[:, : last * PANEL],
+                inverse[last * PANEL - LANES : last * PANEL, : last * PANEL],
+                (((1,), (1,)), ((), ())),
+                precision=lax.Precision.HIGHEST,
+                preferred_element_type=jnp.float32,
+            )
+            send(basis.at[first], basis_out.at[:, last * PANEL - LANES : last * PANEL], 2 * first + 1).start()
+    for t in range(lane_tiles):
+        at = slice(t * LANES, (t + 1) * LANES)
+        send(factor.at[at], factor_out.at[at], 2 * t).wait()
+        send(basis.at[t], basis_out.at[:, at], 2 * t + 1).wait()
 
 
 def finish(sketch, gram, scale):
@@ -586,8 +596,12 @@
             jax.ShapeDtypeStruct(gram.shape, jnp.float32),
         ),
         in_specs=[pl.BlockSpec(memory_space=pltpu.VMEM)] * 2,
-        out_specs=(pl.BlockSpec(memory_space=pltpu.VMEM),) * 2,
-        scratch_shapes=[pltpu.VMEM(gram.shape, jnp.float32)] * 3,
+        out_specs=(pl.BlockSpec(memory_space=pltpu.HBM),) * 2,
+        scratch_shapes=[pltpu.VMEM(gram.shape, jnp.float32)] * 4
+        + [
+            pltpu.VMEM((gram.shape[0] // LANES, sketch.shape[0], LANES), jnp.float32),
+            pltpu.SemaphoreType.DMA((2 * gram.shape[0] // LANES,)),
+        ],
         compiler_params=pltpu.CompilerParams(vmem_limit_bytes=32 << 20),
     )(sketch, gram)
 

time: 86.5 us -> 86.3 us (level)
  no operation moved by 1% of the time
where the time goes in v6:
time: 86.3 us
  Pallas kernels  85.6 us (99%)
    pallas_call x1, Pallas kernels, sketch_and_gram(): pl.pallas_call(functools.partial(kernel, scale), out_shape=(jax.ShapeDtyp...  77.3 us
    pallas_call x1, Pallas kernels, finish(): pl.pallas_call(functools.partial(finish_kernel, scale), out_shape=(jax.Sh...  8.28 us

profile of v6, /device:TPU:1, one launch (start us, length us, event | category | flops | bytes accessed | tf_op | source)
XLA Modules:
  0.0 86.3 jit_solution(17603338734518325922)
XLA Ops:
  0.6 77.3 %shard_map.50 = (f32[128,256]{1,0:T(8,128)S(1)}, f32[32,8,256]{2,1,0:T(8,128)S(1)}) custom-call(s32[1,1,4]{2,1,0:T(1,128)} %lengths.1, bf16[384,8192]{1,0:T(8,128)(2,1)} %bitcast.3, bf16[128,256]{1,0:T(8,128)(2,1)} %probes.1), custom_call_target="tpu_custom_call" | custom-call | tf_op jit(solution)/shard_map/pallas_call | solution.py:416
  78.0 8.3 %shard_map.51 = (f32[128,256]{1,0:T(8,128)}, f32[256,256]{1,0:T(8,128)}) custom-call(f32[128,256]{1,0:T(8,128)S(1)} %get-tuple-element.4.sketch, f32[256,256]{1,0:T(8,128)S(1)} %bitcast.2), custom_call_target="tpu_custom_call" | custom-call | tf_op jit(solution)/shard_map/pallas_call | solution.py:592

commit v7 on v6

--- a/solution.py
+++ b/solution.py
@@ -321,6 +321,7 @@
             for group in groups:
                 tsend2[group, d] = summed(group, d).astype(jnp.bfloat16)
                 scatter_2(group, d).start()
+    for groups in ((2, 3), (0, 1)):
         for group in groups:
             total = summed(group, 0)
             for d in ORDER:

time: 86.3 us -> 85.8 us (level)
  no operation moved by 1% of the time
where the time goes in v7:
time: 85.8 us; the launch traced here: 85.7 us
  Pallas kernels  85.1 us (99%)
    pallas_call x1, Pallas kernels, sketch_and_gram(): pl.pallas_call(functools.partial(kernel, scale), out_shape=(jax.ShapeDtyp...  76.8 us
    pallas_call x1, Pallas kernels, finish(): pl.pallas_call(functools.partial(finish_kernel, scale), out_shape=(jax.Sh...  8.29 us

profile of v7, /device:TPU:1, one launch (start us, length us, event | category | flops | bytes accessed | tf_op | source)
XLA Modules:
  0.0 85.7 jit_solution(12521622116555635833)
XLA Ops:
  0.6 76.8 %shard_map.50 = (f32[128,256]{1,0:T(8,128)S(1)}, f32[32,8,256]{2,1,0:T(8,128)S(1)}) custom-call(s32[1,1,4]{2,1,0:T(1,128)} %lengths.1, bf16[384,8192]{1,0:T(8,128)(2,1)} %bitcast.3, bf16[128,256]{1,0:T(8,128)(2,1)} %probes.1), custom_call_target="tpu_custom_call" | custom-call | tf_op jit(solution)/shard_map/pallas_call | solution.py:417
  77.4 8.3 %shard_map.51 = (f32[128,256]{1,0:T(8,128)}, f32[256,256]{1,0:T(8,128)}) custom-call(f32[128,256]{1,0:T(8,128)S(1)} %get-tuple-element.4.sketch, f32[256,256]{1,0:T(8,128)S(1)} %bitcast.2), custom_call_target="tpu_custom_call" | custom-call | tf_op jit(solution)/shard_map/pallas_call | solution.py:593
